TPU v7x, 32 devices: a whole 2x2x4 slice. The times are simulated.
32 devices in a mesh: tmpl: 8 (over z, y), tm: 4 (over x, core).
Axes of the slice: x: 2, y: 2, z: 4, core: 2. Of those that a mesh axis runs over, the one named last changes fastest.
Arguments:
- records: bfloat16 [8, 64, 2048], P('tmpl', None, 'tm'), may hold values from -80 to 80
- templates: bfloat16 [16, 64, 256], P('tmpl'), may hold values from -6 to 6
Outputs:
- detection: float32 [8, 16, 2048], P(None, 'tmpl', 'tm')
All inputs are finite; a program needn't handle non-finite values.
Results may differ from a plain program's by a relative error of at most 0.0041.
Values may be sent and summed in bfloat16 or wider, within the bound.
A program may use at most 64 MiB of HBM per device.

v0:
```python
import math

import jax
import jax.numpy as jnp
from jax import lax
from jax.sharding import PartitionSpec as P


def passed_along(value, axis, steps):
    count = lax.axis_size(axis)
    first, last = (max(0, -steps), min(count, count - steps))
    return lax.ppermute(value, axis, [(source, source + steps) for source in range(first, last)])


def make_weighted(block):
    wide = block.astype(jnp.float32)
    tinv = lax.rsqrt(jnp.sum(wide * wide, axis=2) + 1e-06)
    weighted = (wide * tinv[:, :, None]).astype(jnp.bfloat16)
    return weighted.reshape(block.shape[0], block.shape[1] * block.shape[2])


def sliding_scale(extended, length):
    count_w, chans, total = extended.shape
    out_len = total - length + 1
    wide = extended.astype(jnp.float32)
    squares = wide * wide
    squares = jnp.concatenate([squares, jnp.zeros((count_w, chans, 1), jnp.float32)], axis=2)
    nblocks = (out_len + length) // 16
    blocks = squares.reshape(count_w, chans, nblocks, 16)
    block_sum = jnp.sum(blocks, axis=3)
    prefix = jnp.cumsum(blocks, axis=3) - blocks
    span = length // 16
    count_b = out_len // 16
    window_sum = block_sum[:, :, 0:count_b]
    for index in range(1, span):
        window_sum = window_sum + block_sum[:, :, index : index + count_b]
    energy = (
        window_sum[:, :, :, None]
        - prefix[:, :, :count_b, :]
        + prefix[:, :, span : span + count_b, :]
    )
    energy = energy.reshape(count_w, chans, out_len)
    return lax.rsqrt(jnp.maximum(energy, 16.0))


def detect(window, window_scale, weighted, length):
    chans, total = window.shape
    out_len = total - length + 1
    width = math.gcd(out_len, 256)
    count = weighted.shape[0]

    def one_part(index):
        begin = index * width
        piece = lax.dynamic_slice_in_dim(window, begin, width + length - 1, 1)
        frames = jnp.stack([piece[:, lag : lag + width] for lag in range(length)], axis=1)
        part_scale = lax.dynamic_slice_in_dim(window_scale, begin, width, 1)
        framed = (frames.astype(jnp.float32) * part_scale[:, None, :]).astype(jnp.bfloat16)
        framed = framed.reshape(chans * length, width)
        return jnp.dot(weighted, framed, preferred_element_type=jnp.float32)

    parts = lax.map(one_part, jnp.arange(out_len // width, dtype=jnp.int32))
    return jnp.transpose(parts, (1, 0, 2)).reshape(count, out_len)


def local(records, templates):
    length = templates.shape[2]
    borrowed = passed_along(records[:, :, : length - 1], "tm", -1)
    extended = jnp.concatenate([records, borrowed], axis=2)
    own_weighted = make_weighted(templates)
    own_scale = sliding_scale(extended, length)[0]
    all_weighted = lax.all_gather(own_weighted, "tmpl", axis=0, tiled=True)
    gathered = detect(extended[0], own_scale, all_weighted, length)[None]
    detection = lax.all_to_all(gathered, "tmpl", split_axis=1, concat_axis=0, tiled=True)
    return detection


def solution(mesh):
    placed = (P("tmpl", None, "tm"), P("tmpl", None, None))
    return jax.shard_map(
        local, mesh=mesh, in_specs=placed, out_specs=P(None, "tmpl", "tm"), check_vma=False
    )
```

profile of v0, /device:TPU:0, one launch (start us, length us, event | category | flops | bytes accessed | tf_op | source)
XLA Modules:
  0.0 488.1 jit_solution(10566786627315098723)
XLA Ops:
  0.0 1.0 copy.288
  1.0 1.3 collective-permute-start
  2.3 0.9 fusion.259
  3.2 0.9 fusion.260
  4.2 33.2 %all-gather = bf16[8,2,16384]{2,1,0:T(2,128)(2,1)S(1)} all-gather(bf16[1,2,16384]{2,1,0:T(2,128)(2,1)S(1)} %reshape.85), channel_id=1, replica_groups=mesh['tmpl'=8,'tm'=4] {'tmpl'}, dimensions={0}, use_global_device_ids=true | all-gather | bytes 589824 | tf_op jit(solution)/shard_map/all_gather | solution.py:71
  37.6 1.7 copy.289
  39.4 29.4 %reduce_window_sum.11 = f32[1,64,48,16]{3,2,1,0:T(8,128)S(1)} reduce-window(f32[1,64,48,16]{3,2,1,0:T(8,128)} %copy.289, f32[]{:T(128)} %constant.6.clone.1), window={size=1x1x1x16 pad=0_0x0_0x0_0x15_0}, to_apply=%region_1.0 | reduce-window | flops 737280 | bytes 393220 | tf_op jit(solution)/shard_map/jit(cumsum)/reduce_window_sum | solution.py:31
  69.8 405.4 %while.10 = (s32[]{:T(128)}, f32[2,16,256]{2,1,0:T(8,128)S(1)}, s32[2]{0:T(128)S(1)}, bf16[64,767]{1,0:T(8,128)(2,1)S(1)}, f32[64,512]{1,0:T(8,128)S(1)}, /*inde...) while((s32[]{:T(128)}, f32[2,16,256]{2,1,0:T(8,128)S(1)}, ...), condition=%wide.region_4.5_spmd, body=%wide.region_3.4_spmd.sunk | while | flops 146800896 | bytes 59463860 | solution.py:61
  71.9 0.7 constant_dynamic-update-slice_fusion.513
  99.3 0.7 constant_dynamic-update-slice_fusion.553
  101.4 0.7 constant_dynamic-update-slice_fusion.556
  107.6 0.7 constant_dynamic-update-slice_fusion.565
  111.0 0.7 constant_dynamic-update-slice_fusion.570
  128.2 0.7 constant_dynamic-update-slice_fusion.595
  130.2 0.7 constant_dynamic-update-slice_fusion.598
  157.7 0.7 constant_dynamic-update-slice_fusion.638
  165.9 0.7 constant_dynamic-update-slice_fusion.650
  169.3 0.7 constant_dynamic-update-slice_fusion.655
  170.7 0.7 constant_dynamic-update-slice_fusion.657
  179.6 0.7 constant_dynamic-update-slice_fusion.670
  180.3 0.7 constant_dynamic-update-slice_fusion.671
  182.4 0.7 constant_dynamic-update-slice_fusion.674
  183.1 0.7 constant_dynamic-update-slice_fusion.675
  184.5 0.7 constant_dynamic-update-slice_fusion.677
  185.9 0.7 constant_dynamic-update-slice_fusion.679
  196.8 0.7 constant_dynamic-update-slice_fusion.695
  206.4 0.7 constant_dynamic-update-slice_fusion.709
  207.8 0.7 constant_dynamic-update-slice_fusion.711
  210.6 0.7 constant_dynamic-update-slice_fusion.715
  222.9 0.7 constant_dynamic-update-slice_fusion.733
  224.3 0.7 constant_dynamic-update-slice_fusion.735
  231.2 0.7 constant_dynamic-update-slice_fusion.745
  239.4 0.7 constant_dynamic-update-slice_fusion.757
  247.0 9.7 %multiply_convert_fusion.2 = bf16[64,256,256]{2,0,1:T(8,128)(2,1)} fusion(bf16[64,256,256]{2,0,1:T(8,128)(2,1)} %constant_dynamic-update-slice_fusion.767, f32[64,256]{1,0:T(8,128)S(1)} %constant_dynamic-slice_fusion.258), kind=kLoop, calls=%fused_computation.clone.1 | loop fusion | flops 12582912 | bytes 16842752 | tf_op jit(solution)/shard_map/while/body/eval_jaxpr/convert_element_type | solution.py:57
  256.6 11.4 %copy.297 = bf16[64,256,256]{2,1,0:T(8,128)(2,1)} copy(bf16[64,256,256]{2,0,1:T(8,128)(2,1)} %multiply_convert_fusion.2) | data formatting | bytes 16777216 | tf_op jit(solution)/shard_map/while/body/eval_jaxpr/convert_element_type | solution.py:57
  268.0 4.6 fusion.271
  274.6 0.7 constant_dynamic-update-slice_fusion.513
  302.0 0.7 constant_dynamic-update-slice_fusion.553
  304.1 0.7 constant_dynamic-update-slice_fusion.556
  313.7 0.7 constant_dynamic-update-slice_fusion.570
  330.9 0.7 constant_dynamic-update-slice_fusion.595
  332.9 0.7 constant_dynamic-update-slice_fusion.598
  360.3 0.7 constant_dynamic-update-slice_fusion.638
  368.6 0.7 constant_dynamic-update-slice_fusion.650
  372.0 0.7 constant_dynamic-update-slice_fusion.655
  373.4 0.7 constant_dynamic-update-slice_fusion.657
  382.3 0.7 constant_dynamic-update-slice_fusion.670
  383.0 0.7 constant_dynamic-update-slice_fusion.671
  385.1 0.7 constant_dynamic-update-slice_fusion.674
  385.8 0.7 constant_dynamic-update-slice_fusion.675
  387.2 0.7 constant_dynamic-update-slice_fusion.677
  388.5 0.7 constant_dynamic-update-slice_fusion.679
  399.5 0.7 constant_dynamic-update-slice_fusion.695
  409.1 0.7 constant_dynamic-update-slice_fusion.709
  410.5 0.7 constant_dynamic-update-slice_fusion.711
  413.3 0.7 constant_dynamic-update-slice_fusion.715
  425.6 0.7 constant_dynamic-update-slice_fusion.733
  427.0 0.7 constant_dynamic-update-slice_fusion.735
  433.9 0.7 constant_dynamic-update-slice_fusion.745
  442.1 0.7 constant_dynamic-update-slice_fusion.757
  449.6 9.7 %multiply_convert_fusion.2 = bf16[64,256,256]{2,0,1:T(8,128)(2,1)} fusion(bf16[64,256,256]{2,0,1:T(8,128)(2,1)} %constant_dynamic-update-slice_fusion.767, f32[64,256]{1,0:T(8,128)S(1)} %constant_dynamic-slice_fusion.258), kind=kLoop, calls=%fused_computation.clone.1 | loop fusion | flops 12582912 | bytes 16842752 | tf_op jit(solution)/shard_map/while/body/eval_jaxpr/convert_element_type | solution.py:57
  459.3 11.4 %copy.297 = bf16[64,256,256]{2,1,0:T(8,128)(2,1)} copy(bf16[64,256,256]{2,0,1:T(8,128)(2,1)} %multiply_convert_fusion.2) | data formatting | bytes 16777216 | tf_op jit(solution)/shard_map/while/body/eval_jaxpr/convert_element_type | solution.py:57
  470.6 4.6 fusion.271
  475.3 12.0 %all_to_all.12 = f32[1,16,512]{2,0,1:T(1,128)S(1)} all-to-all(f32[1,16,512]{2,0,1:T(1,128)S(1)} %broadcast_in_dim_reshape.4), channel_id=1, replica_groups=mesh['tmpl'=8,'tm'=4] {'tmpl'}, dimensions={1} | all-to-all | bytes 65536 | tf_op jit(solution)/shard_map/all_to_all | solution.py:73
  (487 shorter events, 320.7 us)
Async XLA Ops:
  1.0 36.6 %collective-permute-start = (bf16[1,64,255]{1,2,0:T(8,128)(2,1)S(1)}, bf16[1,64,255]{1,2,0:T(8,128)(2,1)S(1)}, u32[]{:S(2)}, u32[]{:S(2)}) collective-permute-start(bf16[1,64,255]{1,2,0:T(8,128)(2,1)S(1)} %slice.844), channel_id=1, source_target_pairs={{1,0},{2,1},{3,2},{5,4},{6,5},{7,6},{9,8},{10,9},{11,10},{13,12},{... | collective-permute-start | bytes 97928 | tf_op jit(solution)/shard_map/ppermute | solution.py:12
where the time goes:
time: 491 us; the launch traced here: 488 us
  local copies, waits for them, and re-layouts  380 us (77%)
  other arithmetic  50.9 us (10%)
  blocking collectives  45.2 us (9%)
  matrix products  9.13 us (2%)
    while x510, local copies, waits for them, and re-layouts  350 us
    all_gather x1, blocking collectives, local(): all_weighted = lax.all_gather(own_weighted, 'tmpl', axis=0, tiled=True)  33.2 us
    another operation x1, other arithmetic, sliding_scale(): prefix = jnp.cumsum(blocks, axis=3) - blocks  29.4 us
    convert_element_type x2, local copies, waits for them, and re-layouts, one_part(): (frames.astype(jnp.float32) * part_scale[:, None, :]).astype(jnp.bfloat16)  22.7 us
    convert_element_type x2, other arithmetic, one_part(): (frames.astype(jnp.float32) * part_scale[:, None, :]).astype(jnp.bfloat16)  19.3 us
    all_to_all x1, blocking collectives, local(): lax.all_to_all(gathered, 'tmpl', split_axis=1, concat_axis=0, tiled=True)  12 us
  transfers between devices with their start and end apart: 1, of which 0 were waited for; matrix products, arithmetic and copies ran while one was open for 0% of the time, Pallas kernels for 0%

commit v1 on v0

v1 whole, which is shorter than its diff:
```python
import functools

import jax
import jax.numpy as jnp
from jax import lax
from jax.experimental import pallas as pl
from jax.experimental.pallas import tpu as pltpu
from jax.sharding import PartitionSpec as P

MESH = pl.DeviceIdType.MESH
LANES = 128


def kernel(
    n, n_tm, rec_ref, tmp_ref, out_ref, wall, wf, ext, xf, scale, g, res,
    wsend, wrecv, hsend, hrecv, osend, orecv,
):
    me = lax.axis_index("tmpl")
    tm = lax.axis_index("tm")
    left = lax.rem(tm + n_tm - 1, n_tm)
    right = lax.rem(tm + 1, n_tm)
    chans, slab = rec_ref.shape
    rows, length = tmp_ref.shape
    own_k = rows // chans
    chunks = (slab + length) // LANES
    halves = length // LANES
    own_blocks = slab // LANES

    barrier = pltpu.get_barrier_semaphore()
    for d in range(1, n):
        pl.semaphore_signal(barrier, inc=1, device_id=(lax.rem(me + d, n), tm), device_id_type=MESH)
    for other in (left, right):
        pl.semaphore_signal(barrier, inc=1, device_id=(me, other), device_id_type=MESH)

    wide = tmp_ref[...].astype(jnp.float32)
    tinv = lax.rsqrt(jnp.sum(wide * wide, axis=1, keepdims=True) + 1e-06)
    weighted = (wide * tinv).astype(jnp.bfloat16)
    row = lax.broadcasted_iota(jnp.int32, (LANES, LANES), 0)
    col = lax.broadcasted_iota(jnp.int32, (LANES, LANES), 1)
    flip = jnp.where(row + col == LANES - 1, 1.0, 0.0).astype(jnp.bfloat16)
    for j in range(halves):
        part = weighted[:, j * LANES : (j + 1) * LANES]
        wall[me, :, j * LANES : (j + 1) * LANES] = jnp.dot(
            part, flip, preferred_element_type=jnp.float32
        ).astype(jnp.bfloat16)

    pl.semaphore_wait(barrier, n + 1)

    halo = pltpu.make_async_remote_copy(
        src_ref=rec_ref.at[:, pl.ds(0, length)], dst_ref=ext, send_sem=hsend, recv_sem=hrecv,
        device_id=(me, left), device_id_type=MESH,
    )
    halo.start()
    sends = []
    for d in range(1, n):
        copy = pltpu.make_async_remote_copy(
            src_ref=wall.at[me], dst_ref=wall.at[me], send_sem=wsend.at[d], recv_sem=wrecv.at[d],
            device_id=(lax.rem(me + d, n), tm), device_id_type=MESH,
        )
        copy.start()
        sends.append(copy)

    keep = col <= row

    def build(first, last):
        def group(index, carry):
            start = pl.multiple_of(index * 8, 8)
            lines = xf[pl.ds(start, 8), first * LANES : (last + 1) * LANES]
            for s in range(8):
                turned = []
                for m in range(last + 1 - first):
                    line = jnp.broadcast_to(lines[s : s + 1, m * LANES : (m + 1) * LANES], (LANES, LANES))
                    turned.append(pltpu.roll(line, 1, 1, stride=1, stride_axis=0))
                for m in range(first, last):
                    block = jnp.where(keep, turned[m - first], turned[m - first + 1])
                    g[start + s, :, m * LANES : (m + 1) * LANES] = block.astype(jnp.bfloat16)
            return carry

        lax.fori_loop(0, chans // 8, group, 0)

    xf[:, :slab] = rec_ref[...].astype(jnp.float32)
    build(0, own_blocks - 1)

    halo.wait()
    borrowed = ext[...].astype(jnp.float32)
    xf[:, slab:] = jnp.where(tm == n_tm - 1, 0.0, borrowed)
    build(own_blocks - 1, chunks - 1)

    def energies(index, carry):
        at = pl.ds(pl.multiple_of(index * 8, 8), 8)
        total = xf[at, :]
        total = total * total
        step = 1
        while step < LANES:
            total = total + pltpu.roll(total, slab + length - step, 1)
            step *= 2
        energy = total[:, :slab]
        for j in range(1, halves):
            energy = energy + total[:, j * LANES : j * LANES + slab]
        scale[at, :] = lax.rsqrt(jnp.maximum(energy, 16.0))
        return carry

    lax.fori_loop(0, chans // 8, energies, 0)

    for d in range(1, n):
        source = lax.rem(me + n - d, n)
        pltpu.make_async_remote_copy(
            src_ref=wall.at[source], dst_ref=wall.at[source], send_sem=wsend.at[d], recv_sem=wrecv.at[d],
            device_id=(source, tm), device_id_type=MESH,
        ).wait_recv()
    for i in range(n):
        for j in range(halves):
            wf[j, i * rows : (i + 1) * rows, :] = wall[i, :, j * LANES : (j + 1) * LANES].astype(jnp.float32)

    def channels(index, acc):
        start = pl.multiple_of(index * 8, 8)
        scales = scale[pl.ds(start, 8), :]
        for s in range(8):
            c = start + s
            lhs = jnp.concatenate(
                [wf[j, pl.ds(c, n * own_k, stride=chans), :] for j in range(halves)], axis=1
            ).astype(jnp.bfloat16)
            frames = jnp.concatenate([g[c, :, j * LANES : j * LANES + slab] for j in range(halves)], axis=0)
            part = jnp.dot(lhs, frames, preferred_element_type=jnp.float32)
            acc = acc + part * scales[s : s + 1, :]
        return acc

    acc = lax.fori_loop(0, chans // 8, channels, jnp.zeros((n * own_k, slab), jnp.float32))
    for i in range(n):
        res[i] = acc[i * own_k : (i + 1) * own_k, :]

    results = []
    for d in range(1, n):
        peer = lax.rem(me + d, n)
        copy = pltpu.make_async_remote_copy(
            src_ref=res.at[peer], dst_ref=out_ref.at[me], send_sem=osend.at[d], recv_sem=orecv.at[d],
            device_id=(peer, tm), device_id_type=MESH,
        )
        copy.start()
        results.append(copy)
    out_ref[me] = res[me]
    for copy in sends:
        copy.wait_send()
    for d in range(1, n):
        results[d - 1].wait_send()
        source = lax.rem(me + n - d, n)
        pltpu.make_async_remote_copy(
            src_ref=res.at[source], dst_ref=out_ref.at[source], send_sem=osend.at[d], recv_sem=orecv.at[d],
            device_id=(source, tm), device_id_type=MESH,
        ).wait_recv()


def solution(mesh):
    n, n_tm = mesh.shape["tmpl"], mesh.shape["tm"]

    def local(records, templates):
        _, chans, slab = records.shape
        own_k, _, length = templates.shape
        rows = own_k * chans
        return pl.pallas_call(
            functools.partial(kernel, n, n_tm),
            out_shape=jax.ShapeDtypeStruct((n, own_k, slab), jnp.float32),
            in_specs=[pl.BlockSpec(memory_space=pltpu.VMEM)] * 2,
            out_specs=pl.BlockSpec(memory_space=pltpu.VMEM),
            scratch_shapes=[
                pltpu.VMEM((n, rows, length), jnp.bfloat16),
                pltpu.VMEM((length // LANES, n * rows, LANES), jnp.float32),
                pltpu.VMEM((chans, length), jnp.bfloat16),
                pltpu.VMEM((chans, slab + length), jnp.float32),
                pltpu.VMEM((chans, slab), jnp.float32),
                pltpu.VMEM((chans, LANES, slab + length - LANES), jnp.bfloat16),
                pltpu.VMEM((n, own_k, slab), jnp.float32),
                pltpu.SemaphoreType.DMA((n,)),
                pltpu.SemaphoreType.DMA((n,)),
                pltpu.SemaphoreType.DMA,
                pltpu.SemaphoreType.DMA,
                pltpu.SemaphoreType.DMA((n,)),
                pltpu.SemaphoreType.DMA((n,)),
            ],
            compiler_params=pltpu.CompilerParams(
                collective_id=0, has_side_effects=True, vmem_limit_bytes=40 * 2**20
            ),
        )(records.reshape(chans, slab), templates.reshape(rows, length))

    placed = (P("tmpl", None, "tm"), P("tmpl", None, None))
    return jax.shard_map(
        local, mesh=mesh, in_specs=placed, out_specs=P(None, "tmpl", "tm"), check_vma=False
    )
```

time: 491 us -> 29.2 us (0.06)
  local copies, waits for them, and re-layouts: 380 us -> 2.3 us
  other arithmetic: 50.9 us -> 0 us
  blocking collectives: 45.2 us -> 0 us
  Pallas kernels: 0 us -> 26.7 us
  matrix products: 9.13 us -> 0 us
    while x512 -> x0, local copies, waits for them, and re-layouts: 350 us -> none
    all_gather x1 -> x0, blocking collectives: 33.2 us -> none  [local(): all_weighted = lax.all_gather(own_weighted, 'tmpl', axis=0, tiled=True)]
    another operation x1 -> x0, other arithmetic: 29.4 us -> none  [sliding_scale(): prefix = jnp.cumsum(blocks, axis=3) - blocks]
    pallas_call x0 -> x1, Pallas kernels: none -> 26.7 us  [local(): pl.pallas_call(functools.partial(kernel, n, n_tm), out_shape=jax.ShapeDty...]
    convert_element_type x2 -> x0, local copies, waits for them, and re-layouts: 22.7 us -> none  [one_part(): (frames.astype(jnp.float32) * part_scale[:, None, :]).astype(jnp.bfloat16)]
    convert_element_type x3 -> x0, other arithmetic: 20.2 us -> none  [the longest x2 19.3 us: one_part(): (frames.astype(jnp.float32) * part_scale[:, None, :]).astype(jnp.bfloat16)]
    all_to_all x1 -> x0, blocking collectives: 12 us -> none  [local(): lax.all_to_all(gathered, 'tmpl', split_axis=1, concat_axis=0, tiled=True)]
    dot_general x2 -> x0, matrix products: 9.13 us -> none  [one_part(): return jnp.dot(weighted, framed, preferred_element_type=jnp.float32)]
  transfers between devices with their start and end apart: 1 -> 0, of which waited for: 0 -> 0; matrix products, arithmetic and copies ran while one was open for 0% -> 0% of each run, Pallas kernels for 0% -> 0%
where the time goes in v1:
time: 29.2 us; the launch traced here: 29 us
  Pallas kernels  26.7 us (91%)
  local copies, waits for them, and re-layouts  2.3 us (8%)
    pallas_call x1, Pallas kernels, local(): pl.pallas_call(functools.partial(kernel, n, n_tm), out_shape=jax.ShapeDty...  26.7 us
    unnamed x5, local copies, waits for them, and re-layouts  2.3 us

profile of v1, /device:TPU:0, one launch (start us, length us, event | category | flops | bytes accessed | tf_op | source)
XLA Modules:
  0.0 29.0 jit_solution(14658710463842149804)
XLA Ops:
  0.0 0.0 copy-start
  0.0 0.8 %copy-done = bf16[1,64,512]{2,1,0:T(8,128)(2,1)S(1)} copy-done((bf16[1,64,512]{2,1,0:T(8,128)(2,1)S(1)}, bf16[1,64,512]{2,1,0:T(8,128)(2,1)}, u32[]{:S(2)}) %copy-start) | copy-done | bytes 65560
  0.8 0.0 copy-start.1
  0.8 0.8 %copy-done.1 = bf16[2,64,256]{2,1,0:T(8,128)(2,1)S(1)} copy-done((bf16[2,64,256]{2,1,0:T(8,128)(2,1)S(1)}, bf16[2,64,256]{2,1,0:T(8,128)(2,1)}, u32[]{:S(2)}) %copy-start.1) | copy-done | bytes 65560
  1.7 26.7 %shard_map.28 = f32[8,2,512]{2,1,0:T(2,128)S(1)} custom-call(bf16[64,512]{1,0:T(8,128)(2,1)S(1)} %bitcast.2, bf16[128,256]{1,0:T(8,128)(2,1)S(1)} %bitcast.3), custom_call_target="tpu_custom_call" | custom-call | tf_op jit(solution)/shard_map/pallas_call | solution.py:160
  28.4 0.6 %copy.4 = f32[8,2,512]{2,1,0:T(2,128)} copy(f32[8,2,512]{2,1,0:T(2,128)S(1)} %shard_map.28) | data formatting | bytes 65536
Async XLA Ops:
  0.0 0.8 %copy-start = (bf16[1,64,512]{2,1,0:T(8,128)(2,1)S(1)}, bf16[1,64,512]{2,1,0:T(8,128)(2,1)}, u32[]{:S(2)}) copy-start(bf16[1,64,512]{2,1,0:T(8,128)(2,1)} %param.2) | copy-start | bytes 196612
  0.8 0.8 %copy-start.1 = (bf16[2,64,256]{2,1,0:T(8,128)(2,1)S(1)}, bf16[2,64,256]{2,1,0:T(8,128)(2,1)}, u32[]{:S(2)}) copy-start(bf16[2,64,256]{2,1,0:T(8,128)(2,1)} %param.3) | copy-start | bytes 196612

commit v2 on v1

v2 whole, which is shorter than its diff:
```python
import functools

import jax
import jax.numpy as jnp
from jax import lax
from jax.experimental import pallas as pl
from jax.experimental.pallas import tpu as pltpu
from jax.sharding import PartitionSpec as P

MESH = pl.DeviceIdType.MESH
LANES = 128
SEED = 128


def kernel(
    n, n_tm, parts, rec_hbm, tmp_hbm, out_ref, rec_ref, tmp_ref, wall, wf, ext, xf, scale, g, res,
    insem, hsend, hrecv, zsend, zrecv, xsend, xrecv, csend, crecv, osend, orecv,
):
    me = lax.axis_index("tmpl")
    tm = lax.axis_index("tm")
    left = lax.rem(tm + n_tm - 1, n_tm)
    right = lax.rem(tm + 1, n_tm)
    chans, slab = rec_ref.shape
    rows, length = tmp_ref.shape
    own_k = rows // chans
    chunks = (slab + length) // LANES
    halves = length // LANES
    own_blocks = slab // LANES

    load_tmp = pltpu.make_async_copy(tmp_hbm, tmp_ref, insem.at[0])
    load_rec = pltpu.make_async_copy(rec_hbm, rec_ref, insem.at[1])
    load_tmp.start()
    load_rec.start()

    core = lax.rem(tm, 2)
    sibling = tm + 1 - 2 * core
    chip = lax.rem(tm // 2, 2)
    across = tm + 2 - 4 * chip
    share = rows // parts
    mine = core if parts == 2 else chip * 2 + core
    theirs = (1 - chip) * 2 + core

    barrier = pltpu.get_barrier_semaphore()
    for d in range(1, n):
        pl.semaphore_signal(barrier, inc=1, device_id=(lax.rem(me + d, n), tm), device_id_type=MESH)
    others = (left, right) if parts == 2 else (left, right, across)
    for other in others:
        pl.semaphore_signal(barrier, inc=1, device_id=(me, other), device_id_type=MESH)

    def block(e):
        return lax.rem(me + n - e, n)

    sent = []

    def piece(which, part, send_sem, recv_sem, to):
        at = wall.at[which, pl.ds(pl.multiple_of(part * share, share), share), :]
        return pltpu.make_async_remote_copy(
            src_ref=at, dst_ref=at, send_sem=send_sem, recv_sem=recv_sem, device_id=to, device_id_type=MESH
        )

    def send(*what):
        copy = piece(*what)
        copy.start()
        sent.append(copy)

    def to_peer(e):
        send(me, mine, zsend.at[e], zrecv.at[e], (lax.rem(me + e, n), tm))

    def to_x(e):
        if parts == 4:
            send(block(e), mine, xsend.at[e], xrecv.at[e], (me, across))

    def to_core(e, part, k):
        i = 2 * e + k
        send(block(e), part, csend.at[i], crecv.at[i], (me, sibling))

    def stage_peers():
        for e in range(1, n):
            to_peer(e)

    def stage_group():
        for e in range(1, n):
            piece(block(e), mine, zsend.at[e], zrecv.at[e], (me, tm)).wait_recv()
            to_x(e)
            to_core(e, mine, 0)

    def stage_core():
        if parts == 4:
            for e in range(1, n):
                piece(block(e), theirs, xsend.at[e], xrecv.at[e], (me, across)).wait_recv()
                to_core(e, theirs, 1)

    def stage_end():
        for e in range(1, n):
            for k in range(parts // 2):
                i = 2 * e + k
                if parts == 2:
                    part = 1 - core
                else:
                    part = (chip if k == 0 else 1 - chip) * 2 + 1 - core
                piece(block(e), part, csend.at[i], crecv.at[i], (me, sibling)).wait_recv()

    load_tmp.wait()
    wide = tmp_ref[...].astype(jnp.float32)
    tinv = lax.rsqrt(jnp.sum(wide * wide, axis=1, keepdims=True) + 1e-06)
    weighted = (wide * tinv).astype(jnp.bfloat16)
    row = lax.broadcasted_iota(jnp.int32, (LANES, LANES), 0)
    col = lax.broadcasted_iota(jnp.int32, (LANES, LANES), 1)
    flip = jnp.where(row + col == LANES - 1, 1.0, 0.0).astype(jnp.bfloat16)
    for j in range(halves):
        part = weighted[:, j * LANES : (j + 1) * LANES]
        wall[me, :, j * LANES : (j + 1) * LANES] = jnp.dot(
            part, flip, preferred_element_type=jnp.float32
        ).astype(jnp.bfloat16)

    pl.semaphore_wait(barrier, n - 1 + len(others))
    stage_peers()
    load_rec.wait()
    halo = pltpu.make_async_remote_copy(
        src_ref=rec_ref.at[:, pl.ds(0, length)], dst_ref=ext, send_sem=hsend, recv_sem=hrecv,
        device_id=(me, left), device_id_type=MESH,
    )
    halo.start()

    seed_row = lax.broadcasted_iota(jnp.int32, (SEED, LANES), 0)
    seed_col = lax.broadcasted_iota(jnp.int32, (SEED, LANES), 1)
    keep = seed_col + (SEED - 1) - seed_row < LANES

    def shifted(pieces, step):
        lane = lax.broadcasted_iota(jnp.int32, pieces[0].shape, 1)
        moved = [pltpu.roll(piece, LANES - step, 1) for piece in pieces]
        last = len(pieces) - 1
        return [jnp.where(lane < LANES - step, moved[m], moved[min(m + 1, last)]) for m in range(last + 1)]

    def frames_of(lines, s, count):
        turned = []
        for m in range(count):
            line = jnp.broadcast_to(lines[s : s + 1, m * LANES : (m + 1) * LANES], (SEED, LANES))
            turned.append(pltpu.roll(line, LANES - SEED + 1, 1, stride=1, stride_axis=0))
        block = [
            jnp.where(keep, turned[m], turned[min(m + 1, count - 1)]).astype(jnp.bfloat16)
            for m in range(count)
        ]
        step = SEED
        while step < LANES:
            ahead = shifted(block, step)
            block = [jnp.concatenate([ahead[m], block[m]], axis=0) for m in range(count)]
            step *= 2
        return block

    def build(start, first, last):
        lines = xf[pl.ds(start, 8), first * LANES : (last + 1) * LANES]
        for s in range(8):
            block = frames_of(lines, s, last + 1 - first)
            for m in range(first, last):
                g[start + s, :, m * LANES : (m + 1) * LANES] = block[m - first]

    def energies():
        total = [xf[:, m * LANES : (m + 1) * LANES] for m in range(chunks)]
        total = [piece * piece for piece in total]
        step = 1
        while step < LANES:
            total = [piece + later for piece, later in zip(total, shifted(total, step))]
            step *= 2
        energy = jnp.concatenate([sum(total[m + 1 : m + halves], total[m]) for m in range(own_blocks)], axis=1)
        scale[...] = lax.rsqrt(jnp.maximum(energy, 16.0))

    def own_part(index, carry):
        build(pl.multiple_of(index * 8, 8), 0, own_blocks - 1)
        return carry

    def rest(index, carry):
        start = pl.multiple_of(index * 8, 8)
        build(start, own_blocks - 1, chunks - 1)
        return carry

    xf[:, :slab] = rec_ref[...].astype(jnp.float32)
    lax.fori_loop(0, chans // 8, own_part, 0)
    halo.wait()
    borrowed = ext[...].astype(jnp.float32)
    xf[:, slab:] = jnp.where(tm == n_tm - 1, 0.0, borrowed)
    lax.fori_loop(0, chans // 8, rest, 0)
    stage_group()
    energies()
    stage_core()
    stage_end()
    for i in range(n):
        for j in range(halves):
            wf[j, i * rows : (i + 1) * rows, :] = wall[i, :, j * LANES : (j + 1) * LANES].astype(jnp.float32)

    def channels(index, acc):
        start = pl.multiple_of(index * 8, 8)
        scales = scale[pl.ds(start, 8), :]
        for s in range(8):
            c = start + s
            lhs = jnp.concatenate(
                [wf[j, pl.ds(c, n * own_k, stride=chans), :] for j in range(halves)], axis=0
            ).astype(jnp.bfloat16)
            sums = jnp.dot(lhs, g[c], preferred_element_type=jnp.float32)
            part = sums[: n * own_k, :slab]
            for j in range(1, halves):
                part = part + sums[j * n * own_k : (j + 1) * n * own_k, j * LANES : j * LANES + slab]
            acc = acc + part * scales[s : s + 1, :]
        return acc

    acc = lax.fori_loop(0, chans // 8, channels, jnp.zeros((n * own_k, slab), jnp.float32))
    for i in range(n):
        res[i] = acc[i * own_k : (i + 1) * own_k, :]

    results = []
    for d in range(1, n):
        peer = lax.rem(me + d, n)
        copy = pltpu.make_async_remote_copy(
            src_ref=res.at[peer], dst_ref=out_ref.at[me], send_sem=osend.at[d], recv_sem=orecv.at[d],
            device_id=(peer, tm), device_id_type=MESH,
        )
        copy.start()
        results.append(copy)
    out_ref[me] = res[me]
    for copy in sent:
        copy.wait_send()
    for d in range(1, n):
        results[d - 1].wait_send()
        source = lax.rem(me + n - d, n)
        pltpu.make_async_remote_copy(
            src_ref=res.at[source], dst_ref=out_ref.at[source], send_sem=osend.at[d], recv_sem=orecv.at[d],
            device_id=(source, tm), device_id_type=MESH,
        ).wait_recv()


def solution(mesh):
    n, n_tm = mesh.shape["tmpl"], mesh.shape["tm"]
    parts = 2

    def local(records, templates):
        _, chans, slab = records.shape
        own_k, _, length = templates.shape
        rows = own_k * chans
        return pl.pallas_call(
            functools.partial(kernel, n, n_tm, parts),
            out_shape=jax.ShapeDtypeStruct((n, own_k, slab), jnp.float32),
            in_specs=[pl.BlockSpec(memory_space=pl.ANY)] * 2,
            out_specs=pl.BlockSpec(memory_space=pltpu.VMEM),
            scratch_shapes=[
                pltpu.VMEM((chans, slab), jnp.bfloat16),
                pltpu.VMEM((rows, length), jnp.bfloat16),
                pltpu.VMEM((n, rows, length), jnp.bfloat16),
                pltpu.VMEM((length // LANES, n * rows, LANES), jnp.float32),
                pltpu.VMEM((chans, length), jnp.bfloat16),
                pltpu.VMEM((chans, slab + length), jnp.float32),
                pltpu.VMEM((chans, slab), jnp.float32),
                pltpu.VMEM((chans, LANES, slab + length - LANES), jnp.bfloat16),
                pltpu.VMEM((n, own_k, slab), jnp.float32),
                pltpu.SemaphoreType.DMA((2,)),
                pltpu.SemaphoreType.DMA,
                pltpu.SemaphoreType.DMA,
                pltpu.SemaphoreType.DMA((n,)),
                pltpu.SemaphoreType.DMA((n,)),
                pltpu.SemaphoreType.DMA((n,)),
                pltpu.SemaphoreType.DMA((n,)),
                pltpu.SemaphoreType.DMA((2 * n,)),
                pltpu.SemaphoreType.DMA((2 * n,)),
                pltpu.SemaphoreType.DMA((n,)),
                pltpu.SemaphoreType.DMA((n,)),
            ],
            compiler_params=pltpu.CompilerParams(
                collective_id=0, has_side_effects=True, vmem_limit_bytes=40 * 2**20
            ),
        )(records.reshape(chans, slab), templates.reshape(rows, length))

    placed = (P("tmpl", None, "tm"), P("tmpl", None, None))
    return jax.shard_map(
        local, mesh=mesh, in_specs=placed, out_specs=P(None, "tmpl", "tm"), check_vma=False
    )
```

time: 29.2 us -> 24.5 us (0.84)
  Pallas kernels: 26.7 us -> 22 us
    pallas_call x1, Pallas kernels: 26.7 us -> 22 us  [local(): pl.pallas_call(functools.partial(kernel, n, n_tm, parts), out_shape=jax.S...]
where the time goes in v2:
time: 24.5 us; the launch traced here: 24.3 us
  Pallas kernels  22 us (90%)
  local copies, waits for them, and re-layouts  2.3 us (9%)
    pallas_call x1, Pallas kernels, local(): pl.pallas_call(functools.partial(kernel, n, n_tm, parts), out_shape=jax.S...  22 us
    unnamed x5, local copies, waits for them, and re-layouts  2.3 us

profile of v2, /device:TPU:0, one launch (start us, length us, event | category | flops | bytes accessed | tf_op | source)
XLA Modules:
  0.0 24.3 jit_solution(2889328340890781057)
XLA Ops:
  0.0 0.0 copy-start
  0.0 0.8 %copy-done = bf16[1,64,512]{2,1,0:T(8,128)(2,1)S(1)} copy-done((bf16[1,64,512]{2,1,0:T(8,128)(2,1)S(1)}, bf16[1,64,512]{2,1,0:T(8,128)(2,1)}, u32[]{:S(2)}) %copy-start) | copy-done | bytes 65560
  0.8 0.0 copy-start.1
  0.8 0.8 %copy-done.1 = bf16[2,64,256]{2,1,0:T(8,128)(2,1)S(1)} copy-done((bf16[2,64,256]{2,1,0:T(8,128)(2,1)S(1)}, bf16[2,64,256]{2,1,0:T(8,128)(2,1)}, u32[]{:S(2)}) %copy-start.1) | copy-done | bytes 65560
  1.7 22.0 %shard_map.28 = f32[8,2,512]{2,1,0:T(2,128)S(1)} custom-call(bf16[64,512]{1,0:T(8,128)(2,1)S(1)} %bitcast.2, bf16[128,256]{1,0:T(8,128)(2,1)S(1)} %bitcast.3), custom_call_target="tpu_custom_call" | custom-call | tf_op jit(solution)/shard_map/pallas_call | solution.py:239
  23.7 0.6 %copy.4 = f32[8,2,512]{2,1,0:T(2,128)} copy(f32[8,2,512]{2,1,0:T(2,128)S(1)} %shard_map.28) | data formatting | bytes 65536
Async XLA Ops:
  0.0 0.8 %copy-start = (bf16[1,64,512]{2,1,0:T(8,128)(2,1)S(1)}, bf16[1,64,512]{2,1,0:T(8,128)(2,1)}, u32[]{:S(2)}) copy-start(bf16[1,64,512]{2,1,0:T(8,128)(2,1)} %param.2) | copy-start | bytes 196612
  0.8 0.8 %copy-start.1 = (bf16[2,64,256]{2,1,0:T(8,128)(2,1)S(1)}, bf16[2,64,256]{2,1,0:T(8,128)(2,1)}, u32[]{:S(2)}) copy-start(bf16[2,64,256]{2,1,0:T(8,128)(2,1)} %param.3) | copy-start | bytes 196612

commit v3 on v2

--- a/solution.py
+++ b/solution.py
@@ -36,7 +36,7 @@
     sibling = tm + 1 - 2 * core
     chip = lax.rem(tm // 2, 2)
     across = tm + 2 - 4 * chip
-    share = rows // parts
+    share = chans // parts
     mine = core if parts == 2 else chip * 2 + core
     theirs = (1 - chip) * 2 + core
 
@@ -53,7 +53,7 @@
     sent = []
 
     def piece(which, part, send_sem, recv_sem, to):
-        at = wall.at[which, pl.ds(pl.multiple_of(part * share, share), share), :]
+        at = wall.at[which, part]
         return pltpu.make_async_remote_copy(
             src_ref=at, dst_ref=at, send_sem=send_sem, recv_sem=recv_sem, device_id=to, device_id_type=MESH
         )
@@ -75,7 +75,7 @@
         send(block(e), part, csend.at[i], crecv.at[i], (me, sibling))
 
     def stage_peers():
-        for e in range(1, n):
+        for e in range(n - 1, 0, -1):
             to_peer(e)
 
     def stage_group():
@@ -90,15 +90,14 @@
                 piece(block(e), theirs, xsend.at[e], xrecv.at[e], (me, across)).wait_recv()
                 to_core(e, theirs, 1)
 
-    def stage_end():
+    def stage_end(k):
         for e in range(1, n):
-            for k in range(parts // 2):
-                i = 2 * e + k
-                if parts == 2:
-                    part = 1 - core
-                else:
-                    part = (chip if k == 0 else 1 - chip) * 2 + 1 - core
-                piece(block(e), part, csend.at[i], crecv.at[i], (me, sibling)).wait_recv()
+            i = 2 * e + k
+            if parts == 2:
+                part = 1 - core
+            else:
+                part = (chip if k == 0 else 1 - chip) * 2 + 1 - core
+            piece(block(e), part, csend.at[i], crecv.at[i], (me, sibling)).wait_recv()
 
     load_tmp.wait()
     wide = tmp_ref[...].astype(jnp.float32)
@@ -109,9 +108,11 @@
     flip = jnp.where(row + col == LANES - 1, 1.0, 0.0).astype(jnp.bfloat16)
     for j in range(halves):
         part = weighted[:, j * LANES : (j + 1) * LANES]
-        wall[me, :, j * LANES : (j + 1) * LANES] = jnp.dot(
-            part, flip, preferred_element_type=jnp.float32
-        ).astype(jnp.bfloat16)
+        turned = jnp.dot(part, flip, preferred_element_type=jnp.float32).astype(jnp.bfloat16)
+        for q in range(parts):
+            for k in range(own_k):
+                at = k * chans + q * share
+                wall[me, q, k * share : (k + 1) * share, j * LANES : (j + 1) * LANES] = turned[at : at + share]
 
     pl.semaphore_wait(barrier, n - 1 + len(others))
     stage_peers()
@@ -174,36 +175,57 @@
         build(start, own_blocks - 1, chunks - 1)
         return carry
 
+    def whole(index, carry):
+        build(pl.multiple_of(index * 8, 8), 0, chunks - 1)
+        return carry
+
     xf[:, :slab] = rec_ref[...].astype(jnp.float32)
-    lax.fori_loop(0, chans // 8, own_part, 0)
+    early = chans // 16
+    lax.fori_loop(0, early, own_part, 0)
     halo.wait()
     borrowed = ext[...].astype(jnp.float32)
     xf[:, slab:] = jnp.where(tm == n_tm - 1, 0.0, borrowed)
-    lax.fori_loop(0, chans // 8, rest, 0)
+    lax.fori_loop(0, early, rest, 0)
+    lax.fori_loop(early, chans // 8, whole, 0)
     stage_group()
     energies()
+
+    size = own_k * share
+
+    def widen(part):
+        for i in range(n):
+            start = pl.multiple_of((part * n + i) * size, size)
+            for j in range(halves):
+                wf[j, pl.ds(start, size), :] = wall[i, part, :, j * LANES : (j + 1) * LANES].astype(jnp.float32)
+
+    def channels(part, index, acc):
+        start = pl.multiple_of(part * share + index * 8, 8)
+        scales = scale[pl.ds(start, 8), :]
+        base = pl.multiple_of(part * n * size + index * 8, 8)
+        for s in range(8):
+            lhs = jnp.concatenate(
+                [wf[j, pl.ds(base + s, n * own_k, stride=share), :] for j in range(halves)], axis=0
+            ).astype(jnp.bfloat16)
+            sums = jnp.dot(lhs, g[start + s], preferred_element_type=jnp.float32)
+            total = sums[: n * own_k, :slab]
+            for j in range(1, halves):
+                total = total + sums[j * n * own_k : (j + 1) * n * own_k, j * LANES : j * LANES + slab]
+            acc = acc + total * scales[s : s + 1, :]
+        return acc
+
+    def correlate(part, acc):
+        widen(part)
+        return lax.fori_loop(0, share // 8, functools.partial(channels, part), acc)
+
+    acc = correlate(mine, jnp.zeros((n * own_k, slab), jnp.float32))
     stage_core()
-    stage_end()
-    for i in range(n):
-        for j in range(halves):
-            wf[j, i * rows : (i + 1) * rows, :] = wall[i, :, j * LANES : (j + 1) * LANES].astype(jnp.float32)
-
-    def channels(index, acc):
-        start = pl.multiple_of(index * 8, 8)
-        scales = scale[pl.ds(start, 8), :]
-        for s in range(8):
-            c = start + s
-            lhs = jnp.concatenate(
-                [wf[j, pl.ds(c, n * own_k, stride=chans), :] for j in range(halves)], axis=0
-            ).astype(jnp.bfloat16)
-            sums = jnp.dot(lhs, g[c], preferred_element_type=jnp.float32)
-            part = sums[: n * own_k, :slab]
-            for j in range(1, halves):
-                part = part + sums[j * n * own_k : (j + 1) * n * own_k, j * LANES : j * LANES + slab]
-            acc = acc + part * scales[s : s + 1, :]
-        return acc
-
-    acc = lax.fori_loop(0, chans // 8, channels, jnp.zeros((n * own_k, slab), jnp.float32))
+    if parts == 4:
+        acc = correlate(theirs, acc)
+    stage_end(0)
+    acc = correlate(1 - core if parts == 2 else chip * 2 + 1 - core, acc)
+    if parts == 4:
+        stage_end(1)
+        acc = correlate((1 - chip) * 2 + 1 - core, acc)
     for i in range(n):
         res[i] = acc[i * own_k : (i + 1) * own_k, :]
 
@@ -244,7 +266,7 @@
             scratch_shapes=[
                 pltpu.VMEM((chans, slab), jnp.bfloat16),
                 pltpu.VMEM((rows, length), jnp.bfloat16),
-                pltpu.VMEM((n, rows, length), jnp.bfloat16),
+                pltpu.VMEM((n, parts, rows // parts, length), jnp.bfloat16),
                 pltpu.VMEM((length // LANES, n * rows, LANES), jnp.float32),
                 pltpu.VMEM((chans, length), jnp.bfloat16),
                 pltpu.VMEM((chans, slab + length), jnp.float32),

time: 24.5 us -> 23.4 us (0.955)
  Pallas kernels: 22 us -> 20.9 us
    pallas_call x1, Pallas kernels: 22 us -> 20.9 us  [local(): pl.pallas_call(functools.partial(kernel, n, n_tm, parts), out_shape=jax.S...]
where the time goes in v3:
time: 23.4 us; the launch traced here: 23.2 us
  Pallas kernels  20.9 us (89%)
  local copies, waits for them, and re-layouts  2.3 us (10%)
    pallas_call x1, Pallas kernels, local(): pl.pallas_call(functools.partial(kernel, n, n_tm, parts), out_shape=jax.S...  20.9 us
    unnamed x5, local copies, waits for them, and re-layouts  2.3 us

profile of v3, /device:TPU:0, one launch (start us, length us, event | category | flops | bytes accessed | tf_op | source)
XLA Modules:
  0.0 23.2 jit_solution(3665073909505312496)
XLA Ops:
  0.0 0.0 copy-start
  0.0 0.8 %copy-done = bf16[1,64,512]{2,1,0:T(8,128)(2,1)S(1)} copy-done((bf16[1,64,512]{2,1,0:T(8,128)(2,1)S(1)}, bf16[1,64,512]{2,1,0:T(8,128)(2,1)}, u32[]{:S(2)}) %copy-start) | copy-done | bytes 65560
  0.8 0.0 copy-start.1
  0.8 0.8 %copy-done.1 = bf16[2,64,256]{2,1,0:T(8,128)(2,1)S(1)} copy-done((bf16[2,64,256]{2,1,0:T(8,128)(2,1)S(1)}, bf16[2,64,256]{2,1,0:T(8,128)(2,1)}, u32[]{:S(2)}) %copy-start.1) | copy-done | bytes 65560
  1.7 20.9 %shard_map.28 = f32[8,2,512]{2,1,0:T(2,128)S(1)} custom-call(bf16[64,512]{1,0:T(8,128)(2,1)S(1)} %bitcast.2, bf16[128,256]{1,0:T(8,128)(2,1)S(1)} %bitcast.3), custom_call_target="tpu_custom_call" | custom-call | tf_op jit(solution)/shard_map/pallas_call | solution.py:261
  22.5 0.6 %copy.4 = f32[8,2,512]{2,1,0:T(2,128)} copy(f32[8,2,512]{2,1,0:T(2,128)S(1)} %shard_map.28) | data formatting | bytes 65536
Async XLA Ops:
  0.0 0.8 %copy-start = (bf16[1,64,512]{2,1,0:T(8,128)(2,1)S(1)}, bf16[1,64,512]{2,1,0:T(8,128)(2,1)}, u32[]{:S(2)}) copy-start(bf16[1,64,512]{2,1,0:T(8,128)(2,1)} %param.2) | copy-start | bytes 196612
  0.8 0.8 %copy-start.1 = (bf16[2,64,256]{2,1,0:T(8,128)(2,1)S(1)}, bf16[2,64,256]{2,1,0:T(8,128)(2,1)}, u32[]{:S(2)}) copy-start(bf16[2,64,256]{2,1,0:T(8,128)(2,1)} %param.3) | copy-start | bytes 196612

commit v4 on v3

--- a/solution.py
+++ b/solution.py
@@ -186,8 +186,8 @@
     borrowed = ext[...].astype(jnp.float32)
     xf[:, slab:] = jnp.where(tm == n_tm - 1, 0.0, borrowed)
     lax.fori_loop(0, early, rest, 0)
+    stage_group()
     lax.fori_loop(early, chans // 8, whole, 0)
-    stage_group()
     energies()
 
     size = own_k * share
@@ -252,7 +252,7 @@
 
 def solution(mesh):
     n, n_tm = mesh.shape["tmpl"], mesh.shape["tm"]
-    parts = 2
+    parts = 4
 
     def local(records, templates):
         _, chans, slab = records.shape

time: 23.4 us -> 23.3 us (level)
  no operation moved by 1% of the time
where the time goes in v4:
time: 23.3 us; the launch traced here: 23.1 us
  Pallas kernels  20.7 us (89%)
  local copies, waits for them, and re-layouts  2.3 us (10%)
    pallas_call x1, Pallas kernels, local(): pl.pallas_call(functools.partial(kernel, n, n_tm, parts), out_shape=jax.S...  20.7 us
    unnamed x5, local copies, waits for them, and re-layouts  2.3 us

profile of v4, /device:TPU:0, one launch (start us, length us, event | category | flops | bytes accessed | tf_op | source)
XLA Modules:
  0.0 23.1 jit_solution(10860017507947386635)
XLA Ops:
  0.0 0.0 copy-start
  0.0 0.8 %copy-done = bf16[1,64,512]{2,1,0:T(8,128)(2,1)S(1)} copy-done((bf16[1,64,512]{2,1,0:T(8,128)(2,1)S(1)}, bf16[1,64,512]{2,1,0:T(8,128)(2,1)}, u32[]{:S(2)}) %copy-start) | copy-done | bytes 65560
  0.8 0.0 copy-start.1
  0.8 0.8 %copy-done.1 = bf16[2,64,256]{2,1,0:T(8,128)(2,1)S(1)} copy-done((bf16[2,64,256]{2,1,0:T(8,128)(2,1)S(1)}, bf16[2,64,256]{2,1,0:T(8,128)(2,1)}, u32[]{:S(2)}) %copy-start.1) | copy-done | bytes 65560
  1.7 20.7 %shard_map.28 = f32[8,2,512]{2,1,0:T(2,128)S(1)} custom-call(bf16[64,512]{1,0:T(8,128)(2,1)S(1)} %bitcast.2, bf16[128,256]{1,0:T(8,128)(2,1)S(1)} %bitcast.3), custom_call_target="tpu_custom_call" | custom-call | tf_op jit(solution)/shard_map/pallas_call | solution.py:261
  22.4 0.6 %copy.4 = f32[8,2,512]{2,1,0:T(2,128)} copy(f32[8,2,512]{2,1,0:T(2,128)S(1)} %shard_map.28) | data formatting | bytes 65536
Async XLA Ops:
  0.0 0.8 %copy-start = (bf16[1,64,512]{2,1,0:T(8,128)(2,1)S(1)}, bf16[1,64,512]{2,1,0:T(8,128)(2,1)}, u32[]{:S(2)}) copy-start(bf16[1,64,512]{2,1,0:T(8,128)(2,1)} %param.2) | copy-start | bytes 196612
  0.8 0.8 %copy-start.1 = (bf16[2,64,256]{2,1,0:T(8,128)(2,1)S(1)}, bf16[2,64,256]{2,1,0:T(8,128)(2,1)}, u32[]{:S(2)}) copy-start(bf16[2,64,256]{2,1,0:T(8,128)(2,1)} %param.3) | copy-start | bytes 196612

commit v5 on v4

--- a/solution.py
+++ b/solution.py
@@ -188,6 +188,7 @@
     lax.fori_loop(0, early, rest, 0)
     stage_group()
     lax.fori_loop(early, chans // 8, whole, 0)
+    stage_core()
     energies()
 
     size = own_k * share
@@ -218,7 +219,6 @@
         return lax.fori_loop(0, share // 8, functools.partial(channels, part), acc)
 
     acc = correlate(mine, jnp.zeros((n * own_k, slab), jnp.float32))
-    stage_core()
     if parts == 4:
         acc = correlate(theirs, acc)
     stage_end(0)

time: 23.3 us -> 24.6 us (1.056)
  Pallas kernels: 20.7 us -> 22.1 us
    pallas_call x1, Pallas kernels: 20.7 us -> 22.1 us  [local(): pl.pallas_call(functools.partial(kernel, n, n_tm, parts), out_shape=jax.S...]
where the time goes in v5:
time: 24.6 us; the launch traced here: 24.4 us
  Pallas kernels  22.1 us (90%)
  local copies, waits for them, and re-layouts  2.3 us (9%)
    pallas_call x1, Pallas kernels, local(): pl.pallas_call(functools.partial(kernel, n, n_tm, parts), out_shape=jax.S...  22.1 us
    unnamed x5, local copies, waits for them, and re-layouts  2.3 us

profile of v5, /device:TPU:0, one launch (start us, length us, event | category | flops | bytes accessed | tf_op | source)
XLA Modules:
  0.0 24.4 jit_solution(6572350200011884491)
XLA Ops:
  0.0 0.0 copy-start
  0.0 0.8 %copy-done = bf16[1,64,512]{2,1,0:T(8,128)(2,1)S(1)} copy-done((bf16[1,64,512]{2,1,0:T(8,128)(2,1)S(1)}, bf16[1,64,512]{2,1,0:T(8,128)(2,1)}, u32[]{:S(2)}) %copy-start) | copy-done | bytes 65560
  0.8 0.0 copy-start.1
  0.8 0.8 %copy-done.1 = bf16[2,64,256]{2,1,0:T(8,128)(2,1)S(1)} copy-done((bf16[2,64,256]{2,1,0:T(8,128)(2,1)S(1)}, bf16[2,64,256]{2,1,0:T(8,128)(2,1)}, u32[]{:S(2)}) %copy-start.1) | copy-done | bytes 65560
  1.7 22.1 %shard_map.28 = f32[8,2,512]{2,1,0:T(2,128)S(1)} custom-call(bf16[64,512]{1,0:T(8,128)(2,1)S(1)} %bitcast.2, bf16[128,256]{1,0:T(8,128)(2,1)S(1)} %bitcast.3), custom_call_target="tpu_custom_call" | custom-call | tf_op jit(solution)/shard_map/pallas_call | solution.py:261
  23.8 0.6 %copy.4 = f32[8,2,512]{2,1,0:T(2,128)} copy(f32[8,2,512]{2,1,0:T(2,128)S(1)} %shard_map.28) | data formatting | bytes 65536
Async XLA Ops:
  0.0 0.8 %copy-start = (bf16[1,64,512]{2,1,0:T(8,128)(2,1)S(1)}, bf16[1,64,512]{2,1,0:T(8,128)(2,1)}, u32[]{:S(2)}) copy-start(bf16[1,64,512]{2,1,0:T(8,128)(2,1)} %param.2) | copy-start | bytes 196612
  0.8 0.8 %copy-start.1 = (bf16[2,64,256]{2,1,0:T(8,128)(2,1)S(1)}, bf16[2,64,256]{2,1,0:T(8,128)(2,1)}, u32[]{:S(2)}) copy-start(bf16[2,64,256]{2,1,0:T(8,128)(2,1)} %param.3) | copy-start | bytes 196612
